TPU v7x, 32 devices: a whole 2x2x4 slice. The times are simulated.
32 devices in a mesh: dp: 2 (over x), expert: 4 (over y, core), mp: 4 (over z).
Axes of the slice: x: 2, y: 2, z: 4, core: 2. Of those that a mesh axis runs over, the one named last changes fastest.
Arguments:
- tokens: bfloat16 [128, 3072], P('dp'), may hold values from -6 to 6
- expert_ids: int32 [128, 2], P('dp'), may hold values from 0 to 3, all different within a row; in each aligned block of 64 rows (0 to 63, 64 to 127, ...) at most 64 rows name the same one
- gate_values: float32 [128, 2], P('dp'), may hold values from 0.2 to 1
- targets: int32 [128], P('dp'), may hold values from 0 to 32767
- w_gate: bfloat16 [4, 3072, 4, 2048], P('expert', None, 'mp', 'dp'), may hold values from -0.109375 to 0.109375
- w_up: bfloat16 [4, 3072, 4, 2048], P('expert', None, 'mp', 'dp'), may hold values from -0.109375 to 0.109375
- w_down: bfloat16 [4, 4, 2048, 3072], P('expert', 'mp', None, 'dp'), may hold values from -0.0625 to 0.0625
- norm_gain: float32 [3072], replicated, may hold values from 0.1 to 1.9
- lens_head: bfloat16 [3072, 32768], P('dp', ('expert', 'mp')), may hold values from -120 to 120
Outputs:
- mixed: bfloat16 [128, 3072], P('dp')
- log_probs: float32 [128], P('dp')
Inputs may be any that keep to these rules, and one draw needn't show every extreme that they name: `expert_ids`: each row names two different experts; in each aligned block of 64 rows no expert is named by more than 64 rows, a bound that some block reaches.
All inputs are finite; a program needn't handle non-finite values.
Results may differ from a plain program's by a relative error of at most 0.0041.
Values may be sent and summed in bfloat16 or wider, within the bound.
A program may use at most 128 MiB of HBM per device.

v0:
```python
import jax
import jax.numpy as jnp
from jax import lax
from jax.sharding import PartitionSpec as P

f32, bf16 = (jnp.float32, jnp.bfloat16)


def per_device(
    tokens, expert_ids, gate_values, targets, w_gate, w_up, w_down, norm_gain, lens_head
):
    rows, feats = tokens.shape
    owner = lax.axis_index("expert")
    weights = jnp.sum(jnp.where(expert_ids == owner, gate_values, f32(0.0)), axis=1)
    gate_mat = w_gate.reshape(feats, -1)
    up_mat = w_up.reshape(feats, -1)
    down_mat = w_down.reshape(w_down.shape[2], w_down.shape[3])
    own_feats = down_mat.shape[1]
    all_tokens = lax.all_gather(tokens, "dp", axis=0, tiled=True)
    all_weights = lax.all_gather(weights, "dp", axis=0, tiled=True)
    gate_part = jnp.dot(all_tokens, gate_mat, preferred_element_type=f32)
    up_part = jnp.dot(all_tokens, up_mat, preferred_element_type=f32)
    hidden = (jax.nn.silu(gate_part) * up_part).astype(bf16)
    hidden = lax.all_gather(hidden, "dp", axis=1, tiled=True)
    part = jnp.dot(hidden, down_mat, preferred_element_type=f32) * all_weights[:, None]
    summed = lax.psum(part, ("expert", "mp"))
    first = lax.axis_index("dp") * own_feats
    own_tokens = lax.dynamic_slice_in_dim(all_tokens, first, own_feats, axis=1)
    own_gain = lax.dynamic_slice_in_dim(norm_gain, first, own_feats, axis=0)
    mixed_part = (own_tokens.astype(f32) + summed).astype(bf16)
    mixed = lax.all_to_all(mixed_part, "dp", split_axis=0, concat_axis=1, tiled=True)
    mixed_f = mixed.astype(f32)
    scale = lax.rsqrt(jnp.mean(mixed_f * mixed_f, axis=1) + 1e-05)
    gained = (mixed_part.astype(f32) * own_gain[None, :]).astype(bf16)
    logits_part = jnp.dot(gained, lens_head, preferred_element_type=f32)
    logits = lax.psum_scatter(logits_part, "dp", scatter_dimension=0, tiled=True)
    logits = logits * scale[:, None]
    vocab_cols = lens_head.shape[1]
    vocab_start = (owner * lax.axis_size("mp") + lax.axis_index("mp")) * vocab_cols
    columns = vocab_start + lax.broadcasted_iota(jnp.int32, (1, vocab_cols), 1)
    hit = columns == targets[:, None]
    target_local = jnp.sum(jnp.where(hit, logits, f32(0.0)), axis=1)
    top = jnp.max(logits, axis=1)
    total = jnp.sum(jnp.exp(logits - top[:, None]), axis=1)
    stats = lax.all_gather(jnp.stack([top, total, target_local]), ("expert", "mp"))
    tops, totals, hits = (stats[:, 0], stats[:, 1], stats[:, 2])
    top_all = jnp.max(tops, axis=0)
    exp_total = jnp.sum(totals * jnp.exp(tops - top_all[None, :]), axis=0)
    log_probs = jnp.sum(hits, axis=0) - top_all - jnp.log(exp_total)
    return (mixed, log_probs)


def solution(mesh):
    in_specs = (
        P("dp", None),
        P("dp", None),
        P("dp", None),
        P("dp"),
        P("expert", None, "mp", "dp"),
        P("expert", None, "mp", "dp"),
        P("expert", "mp", None, "dp"),
        P(),
        P("dp", ("expert", "mp")),
    )
    out_specs = (P("dp", None), P("dp"))
    return jax.shard_map(
        per_device, mesh=mesh, in_specs=in_specs, out_specs=out_specs, check_vma=False
    )
```

profile of v0, /device:TPU:0, one launch (start us, length us, event | category | flops | bytes accessed | tf_op | source)
XLA Modules:
  0.0 207.5 jit_solution(1650163457520954662)
XLA Ops:
  7.2 0.0 all-reduce.3.cloned.1.call-start
  7.2 0.0 slice-start
  7.2 13.1 %all_gather.15 = bf16[128,3072]{1,0:T(8,128)(2,1)S(1)} all-gather(bf16[64,3072]{1,0:T(8,128)(2,1)} %param.9), channel_id=1, replica_groups=mesh['dp'=2,'expert'=4,'mp'=4] {'dp'}, dimensions={0}, use_global_device_ids=true | all-gather | bytes 1179648 | tf_op jit(solution)/shard_map/all_gather | solution.py:19
  20.3 0.0 slice-start.1
  20.3 3.9 %fusion.4 = f32[128,1024]{1,0:T(8,128)S(1)} fusion(bf16[128,3072]{1,0:T(8,128)(2,1)S(1)} %all_gather.15, bf16[1,3072,1,1024]{3,1,2,0:T(8,128)(2,1)} %param.13), kind=kOutput, calls=%fused_computation.4 | convolution fusion | flops 805306368 | bytes 7602176 | tf_op jit(solution)/shard_map/dot_general | solution.py:21
  24.2 0.0 slice-done
  24.2 0.0 slice-done.1
  24.3 0.0 copy-start.4
  24.3 0.0 copy-start.1
  24.3 0.0 copy-start.2
  24.3 1.1 fusion.12
  25.4 8.2 %all_gather.16 = bf16[128,2048]{1,0:T(8,128)(2,1)S(1)} all-gather(bf16[128,1024]{1,0:T(8,128)(2,1)S(1)} %fusion.12), channel_id=1, replica_groups=mesh['dp'=2,'expert'=4,'mp'=4] {'dp'}, dimensions={1}, use_global_device_ids=true | all-gather | bytes 786432 | tf_op jit(solution)/shard_map/all_gather | solution.py:24
  33.6 0.0 copy-done.4
  33.6 0.6 dynamic-slice
  34.8 0.0 copy-done.1
  34.8 0.0 copy-done.2
  34.9 0.2 dynamic-update-slice
  35.1 4.9 %all-reduce = f32[128]{0:T(128)S(1)} all-reduce(f32[128]{0:T(128)S(1)} %dynamic-update-slice), channel_id=1, replica_groups=mesh['dp'=2,'expert'=4,'mp'=4] {'dp'}, use_global_device_ids=true, to_apply=%add | all-reduce | flops 128 | bytes 1024
  40.0 0.0 copy-start
  40.0 4.7 %fusion.6 = f32[128,1536]{1,0:T(8,128)} fusion(bf16[128,2048]{1,0:T(8,128)(2,1)S(1)} %all_gather.16, bf16[1,1,2048,1536]{3,2,1,0:T(8,128)(2,1)} %param.15, f32[128]{0:T(128)S(1)} %all-reduce), kind=kOutput, calls=%fused_computation.6 | convolution fusion | flops 805502976 | bytes 7602688 | tf_op jit(solution)/shard_map/dot_general | solution.py:25
  44.7 0.0 all-reduce.3.cloned.1.call-update
  44.7 0.0 reduce-scatter.2.cloned.1.call-start
  44.8 0.0 copy-done
  44.8 0.1 dynamic_slice.7
  44.9 0.0 copy-start.3
  44.9 93.2 %all-reduce.3.cloned.1.call-done = f32[128,1536]{1,0:T(8,128)} async-done(((f32[128,1536]{1,0:T(8,128)}), f32[128,1536]{1,0:T(8,128)}) %all-reduce.3.cloned.1.call-update) | async-done | bytes 786448 | tf_op jit(solution)/shard_map/psum | solution.py:26
  138.1 1.9 add_convert_fusion
  140.0 4.9 %fusion.15 = f32[128,2048]{1,0:T(8,128)} fusion(bf16[1536,2048]{1,0:T(8,128)(2,1)} %param.17, bf16[128,1536]{1,0:T(8,128)(2,1)} %add_convert_fusion, f32[1536]{0:T(1024)S(1)} %dynamic_slice.7), kind=kOutput, calls=%fused_computation.15 | convolution fusion | flops 805896192 | bytes 7739392 | tf_op jit(solution)/shard_map/dot_general | solution.py:35
  144.9 0.0 reduce-scatter.2.cloned.1.call-update
  145.0 3.5 %all-to-all-start = ((bf16[2,64,1536]{2,1,0:T(8,128)(2,1)}), bf16[2,64,1536]{2,1,0:T(8,128)(2,1)S(1)}, u32[]{:S(2)}, u32[]{:S(2)}) async-start(bf16[2,64,1536]{2,1,0:T(8,128)(2,1)} %bitcast.4), calls=%async_computation | async-start | bytes 786432 | tf_op jit(solution)/shard_map/all_to_all | solution.py:31
  148.5 10.2 %all-to-all-done = bf16[2,64,1536]{2,1,0:T(8,128)(2,1)S(1)} async-done(((bf16[2,64,1536]{2,1,0:T(8,128)(2,1)}), bf16[2,64,1536]{2,1,0:T(8,128)(2,1)S(1)}, u32[]{:S(2)}, u32[]{:S(2)}) %all-to-all-start) | async-done | bytes 393248 | tf_op jit(solution)/shard_map/all_to_all | solution.py:31
  158.6 0.8 copy.16
  159.4 0.2 multiply_reduce_fusion
  159.6 7.2 %reduce-scatter.2.cloned.1.call-done = f32[64,2048]{1,0:T(8,128)} async-done(((f32[128,2048]{1,0:T(8,128)}), f32[64,2048]{1,0:T(8,128)}) %reduce-scatter.2.cloned.1.call-update) | async-done | bytes 524304 | tf_op jit(solution)/shard_map/reduce_scatter | solution.py:36
  166.8 1.2 multiply_reduce_fusion.1
  168.0 0.0 copy-done.3
  168.0 1.4 exponential_reduce_fusion
  169.4 30.6 %all-gather.1 = f32[16,3,64]{2,1,0:T(4,128)S(1)} all-gather(f32[1,3,64]{2,1,0:T(4,128)S(1)} %maximum_bitcast_fusion), channel_id=2, replica_groups=mesh['dp'=2,'expert'=4,'mp'=4] {'expert','mp'}, dimensions={0}, use_global_device_ids=true | all-gather | bytes 13056 | tf_op jit(solution)/shard_map/all_gather | solution.py:45
  200.1 0.5 log_subtract_fusion
  (8 shorter events, 0.1 us)
Async XLA Ops:
  7.2 130.9 %all-reduce.3.cloned.1.call-start = ((), (), s32[]{:S(2)}) async-start(), calls=%async_computation.2 | async-start | bytes 1572864 | tf_op jit(solution)/shard_map/psum | solution.py:26
  7.2 17.0 %slice-start = ((s8[6291456]{0:T(1024)(128)(4,1)}), s8[4194304]{0:T(1024)(128)(4,1)S(1)}, s32[]{:S(2)}) async-start(s8[6291456]{0:T(1024)(128)(4,1)} %bitcast.41), calls=%async_computation.4 | async-start | bytes 8388608
  20.3 3.9 %slice-start.1 = ((s8[6291456]{0:T(1024)(128)(4,1)}), s8[2097152]{0:T(1024)(128)(4,1)S(1)}, s32[]{:S(2)}) async-start(s8[6291456]{0:T(1024)(128)(4,1)} %bitcast.41), calls=%async_computation.5 | async-start | bytes 4194304
  24.3 9.3 %copy-start.4 = (u32[32]{0:T(128)S(1)}, u32[32]{0:T(128)}, u32[]{:S(2)}) copy-start(u32[32]{0:T(128)} %constant.40) | copy-start | bytes 388
  24.3 10.5 %copy-start.1 = (f32[64,2]{0,1:T(2,128)S(1)}, f32[64,2]{0,1:T(2,128)}, u32[]{:S(2)}) copy-start(f32[64,2]{0,1:T(2,128)} %param.11) | copy-start | bytes 1540
  24.3 10.5 %copy-start.2 = (s32[64,2]{0,1:T(2,128)S(1)}, s32[64,2]{0,1:T(2,128)}, u32[]{:S(2)}) copy-start(s32[64,2]{0,1:T(2,128)} %param.10) | copy-start | bytes 1540
  40.0 4.8 %copy-start = (f32[3072]{0:T(1024)S(1)}, f32[3072]{0:T(1024)}, u32[]{:S(2)}) copy-start(f32[3072]{0:T(1024)} %param.16) | copy-start | bytes 36868
  44.7 122.0 %reduce-scatter.2.cloned.1.call-start = ((), (), s32[]{:S(2)}) async-start(), calls=%async_computation.3 | async-start | bytes 1572864 | tf_op jit(solution)/shard_map/reduce_scatter | solution.py:36
  44.9 123.1 %copy-start.3 = (s32[64]{0:T(128)S(1)}, s32[64]{0:T(128)}, u32[]{:S(2)}) copy-start(s32[64]{0:T(128)} %param.12) | copy-start | bytes 772
  145.0 13.7 %all-to-all-start = ((bf16[2,64,1536]{2,1,0:T(8,128)(2,1)}), bf16[2,64,1536]{2,1,0:T(8,128)(2,1)S(1)}, u32[]{:S(2)}, u32[]{:S(2)}) async-start(bf16[2,64,1536]{2,1,0:T(8,128)(2,1)} %bitcast.4), calls=%async_computation | async-start | bytes 786432 | tf_op jit(solution)/shard_map/all_to_all | solution.py:31
Sparse Core Ops, SparseCore 0:
  44.9 93.1 all-reduce.2
  145.1 21.6 reduce-scatter.1
where the time goes:
time: 208 us; the launch traced here: 207 us
  waiting for transfers between devices  111 us (53%)
  blocking collectives  56.8 us (27%)
  between operations  14.9 us (7%)
  matrix products  14.6 us (7%)
  other arithmetic  5.39 us (3%)
  starting transfers between devices  3.56 us (2%)
    psum x1, waiting for transfers between devices, per_device(): summed = lax.psum(part, ('expert', 'mp'))  93.2 us
    all_gather x1, blocking collectives, per_device(): lax.all_gather(jnp.stack([top, total, target_local]), ('expert', 'mp'))  30.6 us
    all_gather x1, blocking collectives, per_device(): all_tokens = lax.all_gather(tokens, 'dp', axis=0, tiled=True)  13.1 us
    all_to_all x1, waiting for transfers between devices, per_device(): lax.all_to_all(mixed_part, 'dp', split_axis=0, concat_axis=1, tiled=True)  10.2 us
    all_gather x1, blocking collectives, per_device(): hidden = lax.all_gather(hidden, 'dp', axis=1, tiled=True)  8.17 us
    reduce_scatter x1, waiting for transfers between devices, per_device(): lax.psum_scatter(logits_part, 'dp', scatter_dimension=0, tiled=True)  7.19 us
    unnamed x1, blocking collectives  4.92 us
    dot_general x1, matrix products, per_device(): logits_part = jnp.dot(gained, lens_head, preferred_element_type=f32)  4.91 us
  transfers between devices with their start and end apart: 3, of which 3 were waited for; matrix products, arithmetic and copies ran while one was open for 1% of the time, Pallas kernels for 0%

commit v1 on v0

--- a/solution.py
+++ b/solution.py
@@ -21,7 +21,19 @@
     gate_part = jnp.dot(all_tokens, gate_mat, preferred_element_type=f32)
     up_part = jnp.dot(all_tokens, up_mat, preferred_element_type=f32)
     hidden = (jax.nn.silu(gate_part) * up_part).astype(bf16)
-    hidden = lax.all_gather(hidden, "dp", axis=1, tiled=True)
+    heard = lax.axis_size("dp")
+    b_next, next_value, after = (heard, lax.axis_index("dp"), hidden.shape[1])
+    formed, w1 = (hidden, 1)
+    while w1 < b_next:
+        formed = jnp.concatenate(
+            [
+                formed,
+                lax.ppermute(formed, "dp", [(num, (num - w1) % b_next) for num in range(b_next)]),
+            ],
+            axis=1,
+        )
+        w1 = 2 * w1
+    hidden = jnp.roll(formed, next_value * after, axis=1)
     part = jnp.dot(hidden, down_mat, preferred_element_type=f32) * all_weights[:, None]
     summed = lax.psum(part, ("expert", "mp"))
     first = lax.axis_index("dp") * own_feats

time: 208 us -> 201 us (0.966)
  blocking collectives: 56.8 us -> 48.6 us
    all_gather x1 -> x0, blocking collectives: 8.17 us -> none  [per_device(): hidden = lax.all_gather(hidden, 'dp', axis=1, tiled=True)]
  transfers between devices with their start and end apart: 3 -> 4, of which waited for: 3 -> 3; matrix products, arithmetic and copies ran while one was open for 1% -> 1% of each run, Pallas kernels for 0% -> 0%
where the time goes in v1:
time: 201 us
  waiting for transfers between devices  110 us (55%)
  blocking collectives  48.6 us (24%)
  matrix products  14.9 us (7%)
  between operations  14.9 us (7%)
  other arithmetic  5.39 us (3%)
  starting transfers between devices  5.36 us (3%)
    psum x1, waiting for transfers between devices, per_device(): summed = lax.psum(part, ('expert', 'mp'))  92.6 us
    all_gather x1, blocking collectives, per_device(): lax.all_gather(jnp.stack([top, total, target_local]), ('expert', 'mp'))  30.6 us
    all_gather x1, blocking collectives, per_device(): all_tokens = lax.all_gather(tokens, 'dp', axis=0, tiled=True)  13.1 us
    all_to_all x1, waiting for transfers between devices, per_device(): lax.all_to_all(mixed_part, 'dp', split_axis=0, concat_axis=1, tiled=True)  10.2 us
    reduce_scatter x1, waiting for transfers between devices, per_device(): lax.psum_scatter(logits_part, 'dp', scatter_dimension=0, tiled=True)  7.19 us
    dot_general x1, matrix products, per_device(): jnp.dot(hidden, down_mat, preferred_element_type=f32) * all_weights[:, None]  5.01 us
    unnamed x1, blocking collectives  4.92 us
    dot_general x1, matrix products, per_device(): logits_part = jnp.dot(gained, lens_head, preferred_element_type=f32)  4.91 us
  transfers between devices with their start and end apart: 4, of which 3 were waited for; matrix products, arithmetic and copies ran while one was open for 1% of the time, Pallas kernels for 0%

profile of v1, /device:TPU:0, one launch (start us, length us, event | category | flops | bytes accessed | tf_op | source)
XLA Modules:
  0.0 200.8 jit_solution(7127057322932538795)
XLA Ops:
  7.2 0.0 all-reduce.3.cloned.1.call-start
  7.2 0.0 slice-start
  7.2 13.1 %all_gather.12 = bf16[128,3072]{1,0:T(8,128)(2,1)S(1)} all-gather(bf16[64,3072]{1,0:T(8,128)(2,1)} %param.9), channel_id=1, replica_groups=mesh['dp'=2,'expert'=4,'mp'=4] {'dp'}, dimensions={0}, use_global_device_ids=true | all-gather | bytes 1179648 | tf_op jit(solution)/shard_map/all_gather | solution.py:19
  20.3 0.0 slice-start.1
  20.3 3.9 %fusion.4 = f32[128,1024]{1,0:T(8,128)S(1)} fusion(bf16[128,3072]{1,0:T(8,128)(2,1)S(1)} %all_gather.12, bf16[1,3072,1,1024]{3,1,2,0:T(8,128)(2,1)} %param.13), kind=kOutput, calls=%fused_computation.4 | convolution fusion | flops 805306368 | bytes 7602176 | tf_op jit(solution)/shard_map/dot_general | solution.py:21
  24.2 0.0 slice-done
  24.2 0.0 slice-done.1
  24.3 0.0 copy-start.4
  24.3 0.0 copy-start.1
  24.3 0.0 copy-start.2
  24.3 1.1 fusion.12
  25.4 0.0 copy-start
  25.4 1.8 collective-permute-start
  27.2 0.0 copy-done.4
  27.2 0.6 dynamic-slice
  28.4 0.0 copy-done.1
  28.4 0.0 copy-done.2
  28.5 0.2 dynamic-update-slice
  28.7 4.9 %all-reduce = f32[128]{0:T(128)S(1)} all-reduce(f32[128]{0:T(128)S(1)} %dynamic-update-slice), channel_id=1, replica_groups=mesh['dp'=2,'expert'=4,'mp'=4] {'dp'}, use_global_device_ids=true, to_apply=%add | all-reduce | flops 128 | bytes 1024
  33.6 0.0 collective-permute-done
  33.6 5.0 %fusion.6 = f32[128,1536]{1,0:T(8,128)} fusion(bf16[1,1,2048,1536]{3,2,1,0:T(8,128)(2,1)} %param.15, s32[]{:T(128)S(6)} %select_n.27, bf16[128,1024]{1,0:T(8,128)(2,1)S(1)} %fusion.12, bf16[128,1024]{1,0:T(8,128)(2,1)S(1)} %collective-permute-done, f32[128]{0:T(128)S(1)} %all-reduce), kind=kOutput, calls=%fused_computation.6 | convolution fusion | flops 807600128 | bytes 7602692 | tf_op jit(solution)/shard_map/dot_general | solution.py:37
  38.7 0.0 all-reduce.3.cloned.1.call-update
  38.7 0.0 reduce-scatter.2.cloned.1.call-start
  38.7 0.0 copy-done
  38.7 0.1 dynamic_slice.12
  38.8 0.0 copy-start.3
  38.8 92.6 %all-reduce.3.cloned.1.call-done = f32[128,1536]{1,0:T(8,128)} async-done(((f32[128,1536]{1,0:T(8,128)}), f32[128,1536]{1,0:T(8,128)}) %all-reduce.3.cloned.1.call-update) | async-done | bytes 786448 | tf_op jit(solution)/shard_map/psum | solution.py:38
  131.5 1.9 add_convert_fusion
  133.4 4.9 %fusion.19 = f32[128,2048]{1,0:T(8,128)} fusion(bf16[1536,2048]{1,0:T(8,128)(2,1)} %param.17, bf16[128,1536]{1,0:T(8,128)(2,1)} %add_convert_fusion, f32[1536]{0:T(1024)S(1)} %dynamic_slice.12), kind=kOutput, calls=%fused_computation.22 | convolution fusion | flops 805896192 | bytes 7739392 | tf_op jit(solution)/shard_map/dot_general | solution.py:47
  138.3 0.0 reduce-scatter.2.cloned.1.call-update
  138.3 3.5 %all-to-all-start = ((bf16[2,64,1536]{2,1,0:T(8,128)(2,1)}), bf16[2,64,1536]{2,1,0:T(8,128)(2,1)S(1)}, u32[]{:S(2)}, u32[]{:S(2)}) async-start(bf16[2,64,1536]{2,1,0:T(8,128)(2,1)} %bitcast.4), calls=%async_computation | async-start | bytes 786432 | tf_op jit(solution)/shard_map/all_to_all | solution.py:43
  141.9 10.2 %all-to-all-done = bf16[2,64,1536]{2,1,0:T(8,128)(2,1)S(1)} async-done(((bf16[2,64,1536]{2,1,0:T(8,128)(2,1)}), bf16[2,64,1536]{2,1,0:T(8,128)(2,1)S(1)}, u32[]{:S(2)}, u32[]{:S(2)}) %all-to-all-start) | async-done | bytes 393248 | tf_op jit(solution)/shard_map/all_to_all | solution.py:43
  152.0 0.8 copy.16
  152.8 0.2 multiply_reduce_fusion
  153.0 7.2 %reduce-scatter.2.cloned.1.call-done = f32[64,2048]{1,0:T(8,128)} async-done(((f32[128,2048]{1,0:T(8,128)}), f32[64,2048]{1,0:T(8,128)}) %reduce-scatter.2.cloned.1.call-update) | async-done | bytes 524304 | tf_op jit(solution)/shard_map/reduce_scatter | solution.py:48
  160.2 1.2 multiply_reduce_fusion.1
  161.4 0.0 copy-done.3
  161.4 1.4 exponential_reduce_fusion
  162.8 30.6 %all-gather.1 = f32[16,3,64]{2,1,0:T(4,128)S(1)} all-gather(f32[1,3,64]{2,1,0:T(4,128)S(1)} %maximum_bitcast_fusion), channel_id=2, replica_groups=mesh['dp'=2,'expert'=4,'mp'=4] {'expert','mp'}, dimensions={0}, use_global_device_ids=true | all-gather | bytes 13056 | tf_op jit(solution)/shard_map/all_gather | solution.py:57
  193.5 0.5 log_subtract_fusion
  (8 shorter events, 0.1 us)
Async XLA Ops:
  7.2 124.3 %all-reduce.3.cloned.1.call-start = ((), (), s32[]{:S(2)}) async-start(), calls=%async_computation.2 | async-start | bytes 1572864 | tf_op jit(solution)/shard_map/psum | solution.py:38
  7.2 17.0 %slice-start = ((s8[6291456]{0:T(1024)(128)(4,1)}), s8[4194304]{0:T(1024)(128)(4,1)S(1)}, s32[]{:S(2)}) async-start(s8[6291456]{0:T(1024)(128)(4,1)} %bitcast.40), calls=%async_computation.4 | async-start | bytes 8388608
  20.3 3.9 %slice-start.1 = ((s8[6291456]{0:T(1024)(128)(4,1)}), s8[2097152]{0:T(1024)(128)(4,1)S(1)}, s32[]{:S(2)}) async-start(s8[6291456]{0:T(1024)(128)(4,1)} %bitcast.40), calls=%async_computation.5 | async-start | bytes 4194304
  24.3 3.0 %copy-start.4 = (u32[32]{0:T(128)S(1)}, u32[32]{0:T(128)}, u32[]{:S(2)}) copy-start(u32[32]{0:T(128)} %constant.62) | copy-start | bytes 388
  24.3 4.2 %copy-start.1 = (f32[64,2]{0,1:T(2,128)S(1)}, f32[64,2]{0,1:T(2,128)}, u32[]{:S(2)}) copy-start(f32[64,2]{0,1:T(2,128)} %param.11) | copy-start | bytes 1540
  24.3 4.2 %copy-start.2 = (s32[64,2]{0,1:T(2,128)S(1)}, s32[64,2]{0,1:T(2,128)}, u32[]{:S(2)}) copy-start(s32[64,2]{0,1:T(2,128)} %param.10) | copy-start | bytes 1540
  25.4 13.3 %copy-start = (f32[3072]{0:T(1024)S(1)}, f32[3072]{0:T(1024)}, u32[]{:S(2)}) copy-start(f32[3072]{0:T(1024)} %param.16) | copy-start | bytes 36868
  25.4 8.2 %collective-permute-start = (bf16[128,1024]{1,0:T(8,128)(2,1)S(1)}, bf16[128,1024]{1,0:T(8,128)(2,1)S(1)}, u32[]{:S(2)}, u32[]{:S(2)}) collective-permute-start(bf16[128,1024]{1,0:T(8,128)(2,1)S(1)} %fusion.12), channel_id=1, source_target_pairs={{0,16},{16,0},{1,17},{17,1},{2,18},{18,2},{3,19},{19,3},{4,20},{20... | collective-permute-start | bytes 786440 | tf_op jit(solution)/shard_map/ppermute | solution.py:31
  38.7 121.5 %reduce-scatter.2.cloned.1.call-start = ((), (), s32[]{:S(2)}) async-start(), calls=%async_computation.3 | async-start | bytes 1572864 | tf_op jit(solution)/shard_map/reduce_scatter | solution.py:48
  38.8 122.6 %copy-start.3 = (s32[64]{0:T(128)S(1)}, s32[64]{0:T(128)}, u32[]{:S(2)}) copy-start(s32[64]{0:T(128)} %param.12) | copy-start | bytes 772
  138.3 13.7 %all-to-all-start = ((bf16[2,64,1536]{2,1,0:T(8,128)(2,1)}), bf16[2,64,1536]{2,1,0:T(8,128)(2,1)S(1)}, u32[]{:S(2)}, u32[]{:S(2)}) async-start(bf16[2,64,1536]{2,1,0:T(8,128)(2,1)} %bitcast.4), calls=%async_computation | async-start | bytes 786432 | tf_op jit(solution)/shard_map/all_to_all | solution.py:43
Sparse Core Ops, SparseCore 0:
  38.8 92.6 all-reduce.2
  138.5 21.6 reduce-scatter.1
